TPU v7x, 32 devices: a whole 2x2x4 slice. The times are simulated.
32 devices in a mesh: groups: 2 (over y), seq: 4 (over z), head: 2 (over x), sub: 2 (over core).
Axes of the slice: x: 2, y: 2, z: 4, core: 2. Of those that a mesh axis runs over, the one named last changes fastest.
Arguments:
- hidden: bfloat16 [4096, 5376], P(('groups', 'seq'), 'sub'), parts along dimension 0, may hold values from -500 to 500
- norm_gain: float32 [5376], replicated, may hold values from 0.25 to 1.75
- w_query: bfloat16 [5376, 4096], P('seq', ('head', 'sub')), may hold values from -0.078125 to 0.078125
- w_key: bfloat16 [5376, 2048], P('seq', ('head', 'sub')), may hold values from -0.078125 to 0.078125
- w_value: bfloat16 [5376, 2048], P('seq', ('head', 'sub')), may hold values from -0.078125 to 0.078125
- query_gain: float32 [128], replicated, may hold values from 1 to 2.5
- key_gain: float32 [128], replicated, may hold values from 1 to 2.5
- block_source: int32 [32], P('groups'), parts along dimension 0, may hold values from 0 to 15, as said below
- block_doc: int32 [32], P('groups'), parts along dimension 0, may hold values from 0 to 3, never falling along the last dimension, each value on 1 to 8 neighbouring positions
Outputs:
- attention: bfloat16 [4096, 4096], P(('groups', 'seq'), ('head', 'sub')), parts along dimension 0
There are 2 independent parts, one for each index of `groups`. A program takes and returns all parts, laid end to end along the dimension named above; an argument that names none is the same for every part. Nothing has to cross between parts.
Inputs may be any that keep to these rules, and one draw needn't show every extreme that they name: block_source[b] is the arrival slot of block b, rows block_source[b] * 128 to block_source[b] * 128 + 127 of hidden, on shard block_source[b] // 4; each slot holds one block. Block b lies on its own shard b // 4 or on the shard just before or just after it. Of one shard's blocks at most 2 lie on each neighbouring shard, exactly as many as that neighbour's blocks lie on it, and in every draw some shard holds exactly 2 blocks of each of its two neighbours. `block_doc`: document ids never fall along the blocks; each document spans 1 to 8 blocks, one exactly 8.
All inputs are finite; a program needn't handle non-finite values.
Results may differ from a plain program's by a relative error of at most 0.012.
Values may be sent and summed in bfloat16 or wider, within the bound.
A program may use at most 128 MiB of HBM per device.

v0:
```python
import jax
import jax.numpy as jnp
from jax import lax
from jax.sharding import PartitionSpec as P

HEAD_DIM = 128
WINDOW = 1024
BLOCK = 128
CAP = 2
QUERY_SCALE = 168.0 ** (-0.5)
EPSILON = 1e-06
ROPE_BASE = 10000.0


def passed_along(x, axis, by):
    size = lax.axis_size(axis)
    pairs = [(i, i + by) for i in range(size) if 0 <= i + by < size]
    return lax.ppermute(x, axis, pairs)


def table_lookup(table, indices):
    hits = indices[:, None] == jnp.arange(table.shape[0], dtype=jnp.int32)[None, :]
    return jnp.sum(jnp.where(hits, table[None, :], 0), axis=1)


def token_positions(block_ids, block_doc):
    first_block = jnp.sum((block_doc[None, :] < block_doc[:, None]).astype(jnp.int32), axis=1)
    start_block = table_lookup(first_block, block_ids)
    within = jnp.arange(BLOCK, dtype=jnp.int32)
    return (
        ((block_ids - start_block)[:, None] * BLOCK + within[None, :])
        .reshape(-1)
        .astype(jnp.float32)
    )


def token_docs(token_ids, block_doc):
    return table_lookup(block_doc, jnp.floor_divide(token_ids, BLOCK))


def head_rotation(values, gain, positions, factor):
    token_count = values.shape[0]
    per_head = values.reshape(token_count, -1, HEAD_DIM)
    normed = (
        per_head * lax.rsqrt(jnp.mean(per_head * per_head, axis=2, keepdims=True) + EPSILON) * gain
    )
    half_dim = HEAD_DIM // 2
    frequency = ROPE_BASE ** (-(jnp.arange(half_dim, dtype=jnp.float32) * 2.0 / HEAD_DIM))
    angles = positions[:, None] * frequency[None, :]
    cosine = jnp.cos(angles)[:, None, :]
    sine_table = jnp.sin(angles)[:, None, :]
    first_half = normed[:, :, :half_dim]
    second_half = normed[:, :, half_dim:]
    turned = jnp.concatenate(
        [
            first_half * cosine - second_half * sine_table,
            second_half * cosine + first_half * sine_table,
        ],
        axis=2,
    )
    return (turned * factor).reshape(token_count, -1).astype(jnp.bfloat16)


def side_ranks(labels):
    length = labels.shape[0]
    earlier = jnp.arange(length)[None, :] < jnp.arange(length)[:, None]
    matching = labels[None, :] == labels[:, None]
    return jnp.sum((earlier & matching).astype(jnp.int32), axis=1)


def outgoing_slots(block_source, target, own_shard, block_count, shard_count):
    first_slot = jnp.clip(target, 0, shard_count - 1) * block_count
    slot_ids = lax.dynamic_slice_in_dim(block_source, first_slot, block_count)
    sending = (slot_ids // block_count == own_shard) & (target >= 0) & (target < shard_count)
    send_rank = side_ranks(sending.astype(jnp.int32))
    wanted = (jnp.arange(CAP)[:, None] == send_rank[None, :]) & sending[None, :]
    return jnp.sum(jnp.where(wanted, (slot_ids % block_count)[None, :], 0), axis=1)


def incoming_index(block_source, own_shard, block_count):
    slot_ids = lax.dynamic_slice_in_dim(block_source, own_shard * block_count, block_count)
    sides = slot_ids // block_count - own_shard
    side_rank = side_ranks(sides)
    from_prior = block_count + side_rank
    from_next = block_count + CAP + side_rank
    return jnp.where(
        sides == 0, slot_ids % block_count, jnp.where(sides < 0, from_prior, from_next)
    )


def migrate(values, block_source, own_shard, shard_count):
    row_count, col_count = values.shape
    block_count = row_count // BLOCK
    pieces = values.reshape(block_count, BLOCK, col_count)
    block_pool = [pieces]
    for offset in (1, -1):
        chosen = outgoing_slots(
            block_source, own_shard + offset, own_shard, block_count, shard_count
        )
        outgoing = jnp.take(pieces, chosen, axis=0)
        block_pool.append(passed_along(outgoing, "seq", offset))
    joined = jnp.concatenate(block_pool, axis=0)
    placed = jnp.take(joined, incoming_index(block_source, own_shard, block_count), axis=0)
    return placed.reshape(row_count, col_count)


def project_rows(halves, norm_gain, w_query, w_key, w_value, query_gain, key_gain, positions):
    full_rows = lax.all_gather(halves, "sub", axis=1, tiled=True)
    as_float = full_rows.astype(jnp.float32)
    normed = (
        as_float
        * lax.rsqrt(jnp.mean(as_float * as_float, axis=1, keepdims=True) + EPSILON)
        * norm_gain
    ).astype(jnp.bfloat16)
    segments = (
        lax.all_gather(w_query, "seq", axis=0, tiled=True),
        lax.all_gather(w_key, "seq", axis=0, tiled=True),
        lax.all_gather(w_value, "seq", axis=0, tiled=True),
    )
    query_raw, key_raw, value_raw = tuple(
        (jnp.dot(normed, segment, preferred_element_type=jnp.float32) for segment in segments)
    )
    query_rot = head_rotation(query_raw, query_gain, positions, QUERY_SCALE)
    key_rot = head_rotation(key_raw, key_gain, positions, 1.0)
    return jnp.concatenate([query_rot, key_rot, value_raw.astype(jnp.bfloat16)], axis=1)


def attend_block(query_rows, key_rows, value_rows, query_tokens, key_tokens, query_docs, key_docs):
    query_count = query_rows.shape[0]
    key_count = key_rows.shape[0]
    kv_count = key_rows.shape[1] // HEAD_DIM
    query_heads = query_rows.reshape(query_count, kv_count, 2, HEAD_DIM)
    key_heads = key_rows.reshape(key_count, kv_count, HEAD_DIM)
    value_heads = value_rows.reshape(key_count, kv_count, HEAD_DIM)
    scores = jnp.einsum(
        "qgjd,kgd->gjqk", query_heads, key_heads, preferred_element_type=jnp.float32
    )
    allowed = (key_tokens[None, :] >= 0) & (key_tokens[None, :] <= query_tokens[:, None])
    allowed = (
        allowed
        & (query_tokens[:, None] - key_tokens[None, :] < WINDOW)
        & (key_docs[None, :] == query_docs[:, None])
    )
    weight_exp = jnp.where(allowed, jnp.exp(scores), 0.0)
    totals = jnp.sum(weight_exp, axis=3)
    summed = jnp.einsum(
        "gjqk,kgd->qgjd",
        weight_exp.astype(jnp.bfloat16),
        value_heads,
        preferred_element_type=jnp.float32,
    )
    return (
        (summed / jnp.transpose(totals, (2, 0, 1))[:, :, :, None])
        .reshape(query_count, -1)
        .astype(jnp.bfloat16)
    )


def body(hidden, norm_gain, w_query, w_key, w_value, query_gain, key_gain, block_source, block_doc):
    row_count = hidden.shape[0]
    block_count = row_count // BLOCK
    own_shard = lax.axis_index("seq")
    shard_count = lax.axis_size("seq")
    own_blocks = own_shard * block_count + jnp.arange(block_count, dtype=jnp.int32)
    moved = migrate(hidden, block_source, own_shard, shard_count)
    packed = project_rows(
        moved,
        norm_gain,
        w_query,
        w_key,
        w_value,
        query_gain,
        key_gain,
        token_positions(own_blocks, block_doc),
    )
    query_width = w_query.shape[1]
    key_width = w_key.shape[1]
    query_rot = packed[:, :query_width]
    key_value = packed[:, query_width:]
    halo_count = max(1, WINDOW // row_count)
    received = []
    for distance in range(halo_count, 0, -1):
        received.append(passed_along(key_value, "seq", distance))
    extended = jnp.concatenate(received + [key_value], axis=0)
    key_all = extended[:, :key_width]
    value_all = extended[:, key_width:]
    query_tokens = own_shard * row_count + jnp.arange(row_count, dtype=jnp.int32)
    key_tokens = own_shard * row_count - WINDOW + jnp.arange(extended.shape[0], dtype=jnp.int32)
    query_docs = token_docs(query_tokens, block_doc)
    key_docs = token_docs(key_tokens, block_doc)
    block_rows = min(512, row_count)

    def one_block(block_index):
        return attend_block(
            query_rot, key_all, value_all, query_tokens, key_tokens, query_docs, key_docs
        )

    result = lax.map(one_block, jnp.arange(row_count // block_rows, dtype=jnp.int32))
    return result.reshape(row_count, -1)


def solution(mesh):
    placed = (
        P(("groups", "seq"), "sub"),
        P(),
        P("seq", ("head", "sub")),
        P("seq", ("head", "sub")),
        P("seq", ("head", "sub")),
        P(),
        P(),
        P("groups"),
        P("groups"),
    )
    return jax.shard_map(
        body,
        mesh=mesh,
        in_specs=placed,
        out_specs=P(("groups", "seq"), ("head", "sub")),
        check_vma=False,
    )
```

profile of v0, /device:TPU:25, one launch (start us, length us, event | category | flops | bytes accessed | tf_op | source)
XLA Modules:
  0.0 590.2 jit_solution(7441517687041226296)
XLA Ops:
  6.5 0.9 fusion.27
  9.1 3.5 gather_fusion.2
  12.6 2.6 broadcast_select_fusion
  15.2 3.2 collective-permute-start.1
  18.5 1.8 gather_fusion.1
  20.3 1.5 broadcast_select_fusion.1
  21.8 1.3 collective-permute-start
  23.2 23.3 %collective-permute-done.1 = bf16[2,128,2688]{2,1,0:T(8,128)(2,1)} collective-permute-done((bf16[2,128,2688]{2,1,0:T(8,128)(2,1)}, bf16[2,128,2688]{2,1,0:T(8,128)(2,1)}, u32[]{:S(2)}, u32[]{:S(2)}) %collective-permute-start.1) | collective-permute-done | bytes 1376288 | tf_op jit(solution)/shard_map/ppermute | solution.py:18
  46.5 8.0 %collective-permute-done = bf16[2,128,2688]{2,1,0:T(8,128)(2,1)S(1)} collective-permute-done((bf16[2,128,2688]{2,1,0:T(8,128)(2,1)S(1)}, bf16[2,128,2688]{2,1,0:T(8,128)(2,1)S(1)}, u32[]{:S(2)}, u32[]{:S(2)}) %collective-permute-start) | collective-permute-done | bytes 1376288 | tf_op jit(solution)/shard_map/ppermute | solution.py:18
  54.4 4.2 pad_maximum_fusion
  58.6 3.5 gather_fusion
  62.1 2.2 bitcast_select_fusion.1
  66.9 1.0 multiply_cosine_fusion
  68.2 14.8 %all-gather.5.cloned.1.call-done = bf16[512,5376]{1,0:T(8,128)(2,1)} async-done(((bf16[512,2688]{1,0:T(8,128)(2,1)}), bf16[512,5376]{1,0:T(8,128)(2,1)}) %all-gather.5.cloned.1.call-update) | async-done | bytes 5505040 | tf_op jit(solution)/shard_map/all_gather | solution.py:108
  83.0 3.7 fusion.6
  86.7 98.0 %all-gather.7.cloned.1.call-done = bf16[5376,512]{1,0:T(8,128)(2,1)} async-done(((bf16[1344,512]{1,0:T(8,128)(2,1)}), bf16[5376,512]{1,0:T(8,128)(2,1)}) %all-gather.7.cloned.1.call-update) | async-done | bytes 5505040 | tf_op jit(solution)/shard_map/all_gather | solution.py:117
  184.7 8.0 %multiply_reduce_fusion.1 = (f32[512,4]{0,1:T(4,128)S(1)}, f32[512,512]{0,1:T(8,128)S(1)}) fusion(bf16[5376,512]{1,0:T(8,128)(2,1)} %all-gather.7.cloned.1.call-done, bf16[512,5376]{1,0:T(8,128)(2,1)} %all-gather.5.cloned.1.call-done, f32[5376]{0:T(1024)S(1)} %copy-done.7, f32[512]{0:T(512)S(1)} %add_rsqrt_fusion.2), kind=kOutput, calls=%fused_computation.34 | convolution fusion | flops 2830104576 | bytes 12090368 | tf_op jit(solution)/shard_map/dot_general | solution.py:121
  193.2 93.9 %all-gather.9.cloned.1.call-done = bf16[5376,512]{1,0:T(8,128)(2,1)} async-done(((bf16[1344,512]{1,0:T(8,128)(2,1)}), bf16[5376,512]{1,0:T(8,128)(2,1)}) %all-gather.9.cloned.1.call-update) | async-done | bytes 5505040 | tf_op jit(solution)/shard_map/all_gather | solution.py:118
  287.0 7.4 %convolution_convert_fusion = bf16[512,512]{0,1:T(8,128)(2,1)S(1)} fusion(bf16[5376,512]{1,0:T(8,128)(2,1)} %all-gather.9.cloned.1.call-done, bf16[512,5376]{1,0:T(8,128)(2,1)} %all-gather.5.cloned.1.call-done, f32[5376]{0:T(1024)S(1)} %copy-done.7, f32[512]{0:T(512)S(1)} %add_rsqrt_fusion.2), kind=kOutput, calls=%fused_computation.31 | convolution fusion | flops 2829844480 | bytes 11557888 | tf_op jit(solution)/shard_map/dot_general | solution.py:121
  294.5 1.3 collective-permute-start.3
  295.8 1.5 collective-permute-start.2
  297.5 2.6 fusion.10
  300.1 55.7 %collective-permute-done.3 = bf16[512,1024]{0,1:T(8,128)(2,1)S(1)} collective-permute-done((bf16[512,1024]{0,1:T(8,128)(2,1)S(1)}, bf16[512,1024]{0,1:T(8,128)(2,1)S(1)}, u32[]{:S(2)}, u32[]{:S(2)}) %collective-permute-start.3) | collective-permute-done | bytes 1048608 | tf_op jit(solution)/shard_map/ppermute | solution.py:18
  355.8 118.7 %collective-permute-done.2 = bf16[512,1024]{0,1:T(8,128)(2,1)S(1)} collective-permute-done((bf16[512,1024]{0,1:T(8,128)(2,1)S(1)}, bf16[512,1024]{0,1:T(8,128)(2,1)S(1)}, u32[]{:S(2)}, u32[]{:S(2)}) %collective-permute-start.2) | collective-permute-done | bytes 1048608 | tf_op jit(solution)/shard_map/ppermute | solution.py:18
  474.5 9.2 %maximum_maximum_fusion = bf16[1536,1024]{0,1:T(8,128)(2,1)S(1)} fusion(bf16[512,512]{0,1:T(8,128)(2,1)S(1)} %convolution_convert_fusion, bf16[512,512]{0,1:T(8,128)(2,1)S(1)} %bitcast.52, bf16[512,1024]{0,1:T(8,128)(2,1)S(1)} %collective-permute-done.3, bf16[512,1024]{0,1:T(8,128)(2,1)S(1)} %collective-permute-done.2), kind=kLoop, calls=%fused_computation.15 | loop fusion | flops 12582912 | bytes 6291456 | tf_op jit(solution)/shard_map/concatenate | solution.py:184
  483.6 1.9 fusion.35
  485.6 59.4 %all-gather.11.cloned.1.call-done = bf16[5376,1024]{1,0:T(8,128)(2,1)} async-done(((bf16[1344,1024]{1,0:T(8,128)(2,1)}), bf16[5376,1024]{1,0:T(8,128)(2,1)}) %all-gather.11.cloned.1.call-update) | async-done | bytes 11010064 | tf_op jit(solution)/shard_map/all_gather | solution.py:116
  545.0 10.3 %convolution_bitcast_fusion = f32[64,8,8,128]{3,1,2,0:T(8,128)S(1)} fusion(bf16[5376,1024]{1,0:T(8,128)(2,1)} %all-gather.11.cloned.1.call-done, bf16[512,5376]{1,0:T(8,128)(2,1)} %all-gather.5.cloned.1.call-done, f32[5376]{0:T(1024)S(1)} %copy-done.7, f32[512]{0:T(512)S(1)} %add_rsqrt_fusion.2), kind=kOutput, calls=%fused_computation.28 | convolution fusion | flops 5648154624 | bytes 18635776 | tf_op jit(solution)/shard_map/dot_general | solution.py:121
  557.5 1.1 multiply_subtract_fusion
  560.3 11.3 %fusion = (f32[4,2,512]{2,1,0:T(2,128)S(1)}, f32[4,1536,512,2]{2,1,3,0:T(8,128)}) fusion(pred[512,1536]{0,1:T(8,128)(4,1)S(1)} %copy-done.3, bf16[1536,4,128,1]{0,2,3,1:T(8,128)(2,1)S(1)} %bitcast.54, bf16[512,4,2,128]{3,0,2,1:T(8,128)(2,1)S(1)} %bitcast.55), kind=kOutput, calls=%fused_computation.4 | convolution fusion | flops 1623191552 | bytes 28590080 | tf_op jit(solution)/shard_map/while/body/eval_jaxpr/qgjd,kgd->gjqk/dot_general | solution.py:135
  571.6 10.7 %fusion.12 = bf16[512,4,2,128]{0,3,2,1:T(8,128)(2,1)S(1)} fusion(bf16[1536,4,128,1]{0,2,3,1:T(8,128)(2,1)S(1)} %bitcast.53, f32[4,1536,512,2]{2,1,3,0:T(8,128)} %get-tuple-element.57, pred[512,1536]{0,1:T(8,128)(4,1)S(1)} %copy-done.3, f32[512,4,2]{0,2,1:T(2,128)S(1)} %bitcast.57), kind=kOutput, calls=%fused_computation.23 | convolution fusion | flops 1624244224 | bytes 28590080 | tf_op jit(solution)/shard_map/while/body/eval_jaxpr/gjqk,kgd->qgjd/dot_general | solution.py:146
  582.3 1.3 copy.36
  (64 shorter events, 8.9 us)
Async XLA Ops:
  6.5 11.9 %copy-start = (bf16[512,2688]{1,0:T(8,128)(2,1)S(1)}, bf16[512,2688]{1,0:T(8,128)(2,1)}, u32[]{:S(2)}) copy-start(bf16[512,2688]{1,0:T(8,128)(2,1)} %param.11) | copy-start | bytes 8257540
  6.5 76.4 %all-gather.5.cloned.1.call-start = ((), (), s32[]{:S(2)}) async-start(), calls=%async_computation | async-start | bytes 8257536 | tf_op jit(solution)/shard_map/all_gather | solution.py:108
  15.2 31.2 %collective-permute-start.1 = (bf16[2,128,2688]{2,1,0:T(8,128)(2,1)}, bf16[2,128,2688]{2,1,0:T(8,128)(2,1)}, u32[]{:S(2)}, u32[]{:S(2)}) collective-permute-start(bf16[2,128,2688]{2,1,0:T(8,128)(2,1)} %broadcast_select_fusion), channel_id=1, source_target_pairs={{4,0},{8,4},{12,8},{5,1},{9,5},{13,9},{6,2},{10,6},{14,10},{7,3},{... | collective-permute-start | bytes 4128776 | tf_op jit(solution)/shard_map/ppermute | solution.py:18
  21.8 32.6 %collective-permute-start = (bf16[2,128,2688]{2,1,0:T(8,128)(2,1)S(1)}, bf16[2,128,2688]{2,1,0:T(8,128)(2,1)S(1)}, u32[]{:S(2)}, u32[]{:S(2)}) collective-permute-start(bf16[2,128,2688]{2,1,0:T(8,128)(2,1)S(1)} %broadcast_select_fusion.1), channel_id=1, source_target_pairs={{0,4},{4,8},{8,12},{1,5},{5,9},{9,13},{2,6},{6,10},{10,14},{3,7},{... | collective-permute-start | bytes 4128776 | tf_op jit(solution)/shard_map/ppermute | solution.py:18
  64.4 2.1 copy-start.4
  64.4 120.3 %all-gather.7.cloned.1.call-start = ((), (), s32[]{:S(2)}) async-start(), calls=%async_computation.1 | async-start | bytes 6881280 | tf_op jit(solution)/shard_map/all_gather | solution.py:117
  65.1 221.9 %all-gather.9.cloned.1.call-start = ((), (), s32[]{:S(2)}) async-start(), calls=%async_computation.2 | async-start | bytes 6881280 | tf_op jit(solution)/shard_map/all_gather | solution.py:118
  65.9 479.1 %all-gather.11.cloned.1.call-start = ((), (), s32[]{:S(2)}) async-start(), calls=%async_computation.3 | async-start | bytes 13762560 | tf_op jit(solution)/shard_map/all_gather | solution.py:116
  67.9 116.8 %copy-start.7 = (f32[5376]{0:T(1024)S(1)}, f32[5376]{0:T(1024)}, u32[]{:S(2)}) copy-start(f32[5376]{0:T(1024)} %param.12) | copy-start | bytes 64516
  86.7 106.0 %copy-start.5 = (f32[128]{0:T(128)S(1)}, f32[128]{0:T(128)}, u32[]{:S(2)}) copy-start(f32[128]{0:T(128)} %param.17) | copy-start | bytes 1540
  294.5 61.3 %collective-permute-start.3 = (bf16[512,1024]{0,1:T(8,128)(2,1)S(1)}, bf16[512,1024]{0,1:T(8,128)(2,1)S(1)}, u32[]{:S(2)}, u32[]{:S(2)}) collective-permute-start(bf16[512,1024]{0,1:T(8,128)(2,1)S(1)} %pad_maximum_fusion.1), channel_id=1, source_target_pairs={{0,4},{4,8},{8,12},{1,5},{5,9},{9,13},{2,6},{6,10},{10,14},{3,7},{... | collective-permute-start | bytes 3145736 | tf_op jit(solution)/shard_map/ppermute | solution.py:18
  295.8 178.7 %collective-permute-start.2 = (bf16[512,1024]{0,1:T(8,128)(2,1)S(1)}, bf16[512,1024]{0,1:T(8,128)(2,1)S(1)}, u32[]{:S(2)}, u32[]{:S(2)}) collective-permute-start(bf16[512,1024]{0,1:T(8,128)(2,1)S(1)} %pad_maximum_fusion.1), channel_id=1, source_target_pairs={{0,8},{4,12},{1,9},{5,13},{2,10},{6,14},{3,11},{7,15},{16,24},{20,... | collective-permute-start | bytes 3145736 | tf_op jit(solution)/shard_map/ppermute | solution.py:18
  555.3 1.4 copy-start.6
  558.6 1.4 copy-start.2
  558.7 1.6 copy-start.3
  560.3 11.3 %copy-start.1 = (bf16[1536,512]{0,1:T(8,128)(2,1)S(1)}, bf16[1536,512]{0,1:T(8,128)(2,1)}, u32[]{:S(2)}) copy-start(bf16[1536,512]{0,1:T(8,128)(2,1)} %get-tuple-element.40) | copy-start | bytes 4718596
Sparse Core Ops, SparseCore 0:
  64.5 18.4 all-gather.4
  84.5 100.1 all-gather.6
  186.3 100.7 all-gather.8
  288.5 256.4 all-gather.10
where the time goes:
time: 591 us; the launch traced here: 590 us
  waiting for transfers between devices  474 us (80%)
  matrix products  47.7 us (8%)
  other arithmetic  33.9 us (6%)
  local copies, waits for them, and re-layouts  14 us (2%)
  between operations  13.5 us (2%)
  starting transfers between devices  7.37 us (1%)
    ppermute x4, waiting for transfers between devices, passed_along(): return lax.ppermute(x, axis, pairs)  206 us
    all_gather x1, waiting for transfers between devices, project_rows(): lax.all_gather(w_key, 'seq', axis=0, tiled=True)  98 us
    all_gather x1, waiting for transfers between devices, project_rows(): lax.all_gather(w_value, 'seq', axis=0, tiled=True)  93.9 us
    all_gather x1, waiting for transfers between devices, project_rows(): lax.all_gather(w_query, 'seq', axis=0, tiled=True)  59.4 us
    dot_general x3, matrix products, project_rows(): jnp.dot(normed, segment, preferred_element_type=jnp.float32)  25.7 us
    all_gather x1, waiting for transfers between devices, project_rows(): full_rows = lax.all_gather(halves, 'sub', axis=1, tiled=True)  14.8 us
  transfers between devices with their start and end apart: 8, of which 8 were waited for; matrix products, arithmetic and copies ran while one was open for 7% of the time, Pallas kernels for 0%

commit v1 on v0

--- a/solution.py
+++ b/solution.py
@@ -10,6 +10,23 @@
 QUERY_SCALE = 168.0 ** (-0.5)
 EPSILON = 1e-06
 ROPE_BASE = 10000.0
+
+
+def _load_series(a0, shard_axis):
+    e_now, top, main = (jax.lax.axis_size(shard_axis), jax.lax.axis_index(shard_axis), a0.shape[0])
+    steps_seen = tuple(((rr, (rr + 1) % e_now) for rr in range(e_now)))
+    pile = tuple(((rr, (rr - 1) % e_now) for rr in range(e_now)))
+    y = jnp.zeros((*a0.shape[:0], e_now * main, *a0.shape[1:]), a0.dtype)
+    front = latest = a0
+    y = lax.dynamic_update_slice_in_dim(y, a0, top * main, axis=0)
+    now = e_now // 2
+    for dev in [*range(1, now + 1)]:
+        front = jax.lax.ppermute(front, shard_axis, steps_seen)
+        y = lax.dynamic_update_slice_in_dim(y, front, (top - dev) % e_now * main, axis=0)
+        if dev < e_now - now:
+            latest = jax.lax.ppermute(latest, shard_axis, pile)
+            y = lax.dynamic_update_slice_in_dim(y, latest, (top + dev) % e_now * main, axis=0)
+    return y
 
 
 def passed_along(x, axis, by):
@@ -114,7 +131,7 @@
     ).astype(jnp.bfloat16)
     segments = (
         lax.all_gather(w_query, "seq", axis=0, tiled=True),
-        lax.all_gather(w_key, "seq", axis=0, tiled=True),
+        _load_series(w_key, shard_axis="seq"),
         lax.all_gather(w_value, "seq", axis=0, tiled=True),
     )
     query_raw, key_raw, value_raw = tuple(

time: 591 us -> 548 us (0.927)
  waiting for transfers between devices: 474 us -> 419 us
  local copies, waits for them, and re-layouts: 14 us -> 25.9 us
    ppermute x0 -> x3, waiting for transfers between devices: none -> 137 us  [the longest x2 89.3 us: _load_series(): front = jax.lax.ppermute(front, shard_axis, steps_seen)]
    all_gather x1 -> x0, waiting for transfers between devices: 98 us -> none  [project_rows(): lax.all_gather(w_key, 'seq', axis=0, tiled=True)]
    all_gather x1, waiting for transfers between devices: 93.9 us -> 16.6 us  [project_rows(): lax.all_gather(w_value, 'seq', axis=0, tiled=True)]
    all_gather x1, waiting for transfers between devices: 14.8 us -> 0.01 us  [project_rows(): full_rows = lax.all_gather(halves, 'sub', axis=1, tiled=True)]
    dynamic_update_slice x0 -> x4, local copies, waits for them, and re-layouts: none -> 8.81 us  [the longest x2 5.09 us: _load_series(): lax.dynamic_update_slice_in_dim(y, front, (top - dev) % e_now * main, axi...]
  transfers between devices with their start and end apart: 8 -> 10, of which waited for: 8 -> 9; matrix products, arithmetic and copies ran while one was open for 7% -> 9% of each run, Pallas kernels for 0% -> 0%
where the time goes in v1:
time: 548 us
  waiting for transfers between devices  419 us (76%)
  matrix products  45.6 us (8%)
  other arithmetic  34.1 us (6%)
  local copies, waits for them, and re-layouts  25.9 us (5%)
  between operations  13.5 us (2%)
  starting transfers between devices  10.2 us (2%)
    ppermute x4, waiting for transfers between devices, passed_along(): return lax.ppermute(x, axis, pairs)  204 us
    ppermute x2, waiting for transfers between devices, _load_series(): front = jax.lax.ppermute(front, shard_axis, steps_seen)  89.3 us
    all_gather x1, waiting for transfers between devices, project_rows(): lax.all_gather(w_query, 'seq', axis=0, tiled=True)  60 us
    ppermute x1, waiting for transfers between devices, _load_series(): latest = jax.lax.ppermute(latest, shard_axis, pile)  47.4 us
    dot_general x3, matrix products, project_rows(): jnp.dot(normed, segment, preferred_element_type=jnp.float32)  23.5 us
    all_gather x1, waiting for transfers between devices, project_rows(): lax.all_gather(w_value, 'seq', axis=0, tiled=True)  16.6 us
    dot_general x1, matrix products, attend_block(): jnp.einsum('qgjd,kgd->gjqk', query_heads, key_heads, preferred_element_ty...  11.4 us
  transfers between devices with their start and end apart: 10, of which 9 were waited for; matrix products, arithmetic and copies ran while one was open for 9% of the time, Pallas kernels for 0%

profile of v1, /device:TPU:25, one launch (start us, length us, event | category | flops | bytes accessed | tf_op | source)
XLA Modules:
  0.0 547.9 jit_solution(1554839180911790925)
XLA Ops:
  9.1 3.5 gather_fusion.2
  12.6 2.6 broadcast_select_fusion
  15.2 3.2 collective-permute-start.1
  18.5 1.8 gather_fusion.1
  20.3 1.5 broadcast_select_fusion.1
  23.2 23.3 %collective-permute-done.1 = bf16[2,128,2688]{2,1,0:T(8,128)(2,1)} collective-permute-done((bf16[2,128,2688]{2,1,0:T(8,128)(2,1)}, bf16[2,128,2688]{2,1,0:T(8,128)(2,1)}, u32[]{:S(2)}, u32[]{:S(2)}) %collective-permute-start.1) | collective-permute-done | bytes 1376288 | tf_op jit(solution)/shard_map/ppermute | solution.py:35
  46.5 8.0 %collective-permute-done = bf16[2,128,2688]{2,1,0:T(8,128)(2,1)S(1)} collective-permute-done((bf16[2,128,2688]{2,1,0:T(8,128)(2,1)S(1)}, bf16[2,128,2688]{2,1,0:T(8,128)(2,1)S(1)}, u32[]{:S(2)}, u32[]{:S(2)}) %collective-permute-start) | collective-permute-done | bytes 1376288 | tf_op jit(solution)/shard_map/ppermute | solution.py:35
  54.4 4.2 pad_maximum_fusion
  58.6 3.5 gather_fusion
  62.1 2.2 bitcast_select_fusion.1
  65.9 1.5 collective-permute-start.3
  67.8 28.8 %collective-permute-done.2 = bf16[1344,512]{1,0:T(8,128)(2,1)} collective-permute-done((bf16[1344,512]{1,0:T(8,128)(2,1)S(1)}, bf16[1344,512]{1,0:T(8,128)(2,1)}, u32[]{:S(2)}, u32[]{:S(2)}) %collective-permute-start.2) | collective-permute-done | bytes 1376288 | tf_op jit(solution)/shard_map/ppermute | solution.py:24
  99.3 2.8 broadcast_in_dim.164
  103.3 2.6 constant_dynamic-update-slice_fusion.2
  105.8 47.4 %collective-permute-done.3 = bf16[1344,512]{1,0:T(8,128)(2,1)} collective-permute-done((bf16[1344,512]{1,0:T(8,128)(2,1)S(1)}, bf16[1344,512]{1,0:T(8,128)(2,1)}, u32[]{:S(2)}, u32[]{:S(2)}) %collective-permute-start.3) | collective-permute-done | bytes 1376288 | tf_op jit(solution)/shard_map/ppermute | solution.py:27
  153.3 2.6 constant_dynamic-update-slice_fusion.1
  155.8 60.5 %collective-permute-done.4 = bf16[1344,512]{1,0:T(8,128)(2,1)} collective-permute-done((bf16[1344,512]{1,0:T(8,128)(2,1)}, bf16[1344,512]{1,0:T(8,128)(2,1)}, u32[]{:S(2)}, u32[]{:S(2)}) %collective-permute-start.4) | collective-permute-done | bytes 1376288 | tf_op jit(solution)/shard_map/ppermute | solution.py:24
  216.3 2.5 constant_dynamic-update-slice_fusion
  218.8 3.9 fusion.6
  223.0 5.8 %multiply_reduce_fusion.1 = (f32[512,4]{0,1:T(4,128)S(1)}, f32[512,512]{0,1:T(8,128)S(1)}) fusion(bf16[5376,512]{1,0:T(8,128)(2,1)} %constant_dynamic-update-slice_fusion, bf16[512,5376]{1,0:T(8,128)(2,1)S(1)} %copy-done.1, f32[5376]{0:T(1024)S(1)} %copy-done.9, f32[512]{0:T(512)S(1)} %add_rsqrt_fusion.2), kind=kOutput, calls=%fused_computation.34 | convolution fusion | flops 2830104576 | bytes 12090368 | tf_op jit(solution)/shard_map/dot_general | solution.py:138
  229.3 16.6 %all-gather.6.cloned.1.call-done = bf16[5376,512]{1,0:T(8,128)(2,1)} async-done(((bf16[1344,512]{1,0:T(8,128)(2,1)}), bf16[5376,512]{1,0:T(8,128)(2,1)}) %all-gather.6.cloned.1.call-update) | async-done | bytes 5505040 | tf_op jit(solution)/shard_map/all_gather | solution.py:135
  245.9 7.3 %convolution_convert_fusion = bf16[512,512]{0,1:T(8,128)(2,1)S(1)} fusion(bf16[5376,512]{1,0:T(8,128)(2,1)} %all-gather.6.cloned.1.call-done, bf16[512,5376]{1,0:T(8,128)(2,1)} %all-gather.4.cloned.1.call-done, f32[5376]{0:T(1024)S(1)} %copy-done.9, f32[512]{0:T(512)S(1)} %add_rsqrt_fusion.2), kind=kOutput, calls=%fused_computation.31 | convolution fusion | flops 2829844480 | bytes 11557888 | tf_op jit(solution)/shard_map/dot_general | solution.py:138
  254.6 1.5 collective-permute-start.5
  256.4 2.6 fusion.10
  259.0 55.0 %collective-permute-done.6 = bf16[512,1024]{0,1:T(8,128)(2,1)S(1)} collective-permute-done((bf16[512,1024]{0,1:T(8,128)(2,1)S(1)}, bf16[512,1024]{0,1:T(8,128)(2,1)S(1)}, u32[]{:S(2)}, u32[]{:S(2)}) %collective-permute-start.6) | collective-permute-done | bytes 1048608 | tf_op jit(solution)/shard_map/ppermute | solution.py:35
  314.0 117.6 %collective-permute-done.5 = bf16[512,1024]{0,1:T(8,128)(2,1)S(1)} collective-permute-done((bf16[512,1024]{0,1:T(8,128)(2,1)S(1)}, bf16[512,1024]{0,1:T(8,128)(2,1)S(1)}, u32[]{:S(2)}, u32[]{:S(2)}) %collective-permute-start.5) | collective-permute-done | bytes 1048608 | tf_op jit(solution)/shard_map/ppermute | solution.py:35
  431.6 9.2 %maximum_maximum_fusion = bf16[1536,1024]{0,1:T(8,128)(2,1)S(1)} fusion(bf16[512,512]{0,1:T(8,128)(2,1)S(1)} %convolution_convert_fusion, bf16[512,512]{0,1:T(8,128)(2,1)S(1)} %bitcast.52, bf16[512,1024]{0,1:T(8,128)(2,1)S(1)} %collective-permute-done.6, bf16[512,1024]{0,1:T(8,128)(2,1)S(1)} %collective-permute-done.5), kind=kLoop, calls=%fused_computation.15 | loop fusion | flops 12582912 | bytes 6291456 | tf_op jit(solution)/shard_map/concatenate | solution.py:201
  440.7 1.9 fusion.35
  442.7 60.0 %all-gather.8.cloned.1.call-done = bf16[5376,1024]{1,0:T(8,128)(2,1)} async-done(((bf16[1344,1024]{1,0:T(8,128)(2,1)}), bf16[5376,1024]{1,0:T(8,128)(2,1)}) %all-gather.8.cloned.1.call-update) | async-done | bytes 11010064 | tf_op jit(solution)/shard_map/all_gather | solution.py:133
  502.7 10.3 %convolution_bitcast_fusion = f32[64,8,8,128]{3,1,2,0:T(8,128)S(1)} fusion(bf16[5376,1024]{1,0:T(8,128)(2,1)} %all-gather.8.cloned.1.call-done, bf16[512,5376]{1,0:T(8,128)(2,1)} %all-gather.4.cloned.1.call-done, f32[5376]{0:T(1024)S(1)} %copy-done.9, f32[512]{0:T(512)S(1)} %add_rsqrt_fusion.2), kind=kOutput, calls=%fused_computation.28 | convolution fusion | flops 5648154624 | bytes 18635776 | tf_op jit(solution)/shard_map/dot_general | solution.py:138
  518.0 11.4 %fusion = (f32[4,2,512]{2,1,0:T(2,128)S(1)}, f32[4,1536,512,2]{2,1,3,0:T(8,128)}) fusion(pred[512,1536]{0,1:T(8,128)(4,1)S(1)} %copy-done.5, bf16[1536,4,128,1]{0,2,3,1:T(8,128)(2,1)S(1)} %bitcast.54, bf16[512,4,2,128]{3,0,2,1:T(8,128)(2,1)S(1)} %bitcast.55), kind=kOutput, calls=%fused_computation.4 | convolution fusion | flops 1623191552 | bytes 28590080 | tf_op jit(solution)/shard_map/while/body/eval_jaxpr/qgjd,kgd->gjqk/dot_general | solution.py:152
  529.4 10.7 %fusion.12 = bf16[512,4,2,128]{0,3,2,1:T(8,128)(2,1)S(1)} fusion(bf16[1536,4,128,1]{0,2,3,1:T(8,128)(2,1)S(1)} %bitcast.53, f32[4,1536,512,2]{2,1,3,0:T(8,128)} %get-tuple-element.57, pred[512,1536]{0,1:T(8,128)(4,1)S(1)} %copy-done.5, f32[512,4,2]{0,2,1:T(2,128)S(1)} %bitcast.57), kind=kOutput, calls=%fused_computation.23 | convolution fusion | flops 1624244224 | bytes 28590080 | tf_op jit(solution)/shard_map/while/body/eval_jaxpr/gjqk,kgd->qgjd/dot_general | solution.py:163
  (76 shorter events, 18.1 us)
Async XLA Ops:
  6.5 11.9 %copy-start = (bf16[512,2688]{1,0:T(8,128)(2,1)S(1)}, bf16[512,2688]{1,0:T(8,128)(2,1)}, u32[]{:S(2)}) copy-start(bf16[512,2688]{1,0:T(8,128)(2,1)} %param.11) | copy-start | bytes 8257540
  6.5 212.3 %all-gather.4.cloned.1.call-start = ((), (), s32[]{:S(2)}) async-start(), calls=%async_computation | async-start | bytes 8257536 | tf_op jit(solution)/shard_map/all_gather | solution.py:125
  15.2 31.2 %collective-permute-start.1 = (bf16[2,128,2688]{2,1,0:T(8,128)(2,1)}, bf16[2,128,2688]{2,1,0:T(8,128)(2,1)}, u32[]{:S(2)}, u32[]{:S(2)}) collective-permute-start(bf16[2,128,2688]{2,1,0:T(8,128)(2,1)} %broadcast_select_fusion), channel_id=1, source_target_pairs={{4,0},{8,4},{12,8},{5,1},{9,5},{13,9},{6,2},{10,6},{14,10},{7,3},{... | collective-permute-start | bytes 4128776 | tf_op jit(solution)/shard_map/ppermute | solution.py:35
  21.8 32.6 %collective-permute-start = (bf16[2,128,2688]{2,1,0:T(8,128)(2,1)S(1)}, bf16[2,128,2688]{2,1,0:T(8,128)(2,1)S(1)}, u32[]{:S(2)}, u32[]{:S(2)}) collective-permute-start(bf16[2,128,2688]{2,1,0:T(8,128)(2,1)S(1)} %broadcast_select_fusion.1), channel_id=1, source_target_pairs={{0,4},{4,8},{8,12},{1,5},{5,9},{9,13},{2,6},{6,10},{10,14},{3,7},{... | collective-permute-start | bytes 4128776 | tf_op jit(solution)/shard_map/ppermute | solution.py:35
  64.3 1.5 copy-start.4
  64.3 3.0 copy-start.6
  64.4 181.5 %all-gather.6.cloned.1.call-start = ((), (), s32[]{:S(2)}) async-start(), calls=%async_computation.1 | async-start | bytes 6881280 | tf_op jit(solution)/shard_map/all_gather | solution.py:135
  65.1 437.6 %all-gather.8.cloned.1.call-start = ((), (), s32[]{:S(2)}) async-start(), calls=%async_computation.2 | async-start | bytes 13762560 | tf_op jit(solution)/shard_map/all_gather | solution.py:133
  65.9 30.8 %collective-permute-start.2 = (bf16[1344,512]{1,0:T(8,128)(2,1)S(1)}, bf16[1344,512]{1,0:T(8,128)(2,1)}, u32[]{:S(2)}, u32[]{:S(2)}) collective-permute-start(bf16[1344,512]{1,0:T(8,128)(2,1)S(1)} %copy-done.4), channel_id=1, source_target_pairs={{0,4},{4,8},{8,12},{12,0},{1,5},{5,9},{9,13},{13,1},{2,6},{6,10},{... | collective-permute-start | bytes 4128776 | tf_op jit(solution)/shard_map/ppermute | solution.py:24
  65.9 87.3 %collective-permute-start.3 = (bf16[1344,512]{1,0:T(8,128)(2,1)S(1)}, bf16[1344,512]{1,0:T(8,128)(2,1)}, u32[]{:S(2)}, u32[]{:S(2)}) collective-permute-start(bf16[1344,512]{1,0:T(8,128)(2,1)S(1)} %copy-done.4), channel_id=1, source_target_pairs={{0,12},{4,0},{8,4},{12,8},{1,13},{5,1},{9,5},{13,9},{2,14},{6,2},{... | collective-permute-start | bytes 4128776 | tf_op jit(solution)/shard_map/ppermute | solution.py:27
  96.7 119.6 %collective-permute-start.4 = (bf16[1344,512]{1,0:T(8,128)(2,1)}, bf16[1344,512]{1,0:T(8,128)(2,1)}, u32[]{:S(2)}, u32[]{:S(2)}) collective-permute-start(bf16[1344,512]{1,0:T(8,128)(2,1)} %collective-permute-done.2), channel_id=1, source_target_pairs={{0,4},{4,8},{8,12},{12,0},{1,5},{5,9},{9,13},{13,1},{2,6},{6,10},{... | collective-permute-start | bytes 4128776 | tf_op jit(solution)/shard_map/ppermute | solution.py:24
  216.3 6.4 %copy-start.9 = (f32[5376]{0:T(1024)S(1)}, f32[5376]{0:T(1024)}, u32[]{:S(2)}) copy-start(f32[5376]{0:T(1024)} %param.12) | copy-start | bytes 64516
  218.8 4.2 copy-start.1
  223.0 5.9 %copy-start.7 = (f32[128]{0:T(128)S(1)}, f32[128]{0:T(128)}, u32[]{:S(2)}) copy-start(f32[128]{0:T(128)} %param.17) | copy-start | bytes 1540
  253.3 60.7 %collective-permute-start.6 = (bf16[512,1024]{0,1:T(8,128)(2,1)S(1)}, bf16[512,1024]{0,1:T(8,128)(2,1)S(1)}, u32[]{:S(2)}, u32[]{:S(2)}) collective-permute-start(bf16[512,1024]{0,1:T(8,128)(2,1)S(1)} %pad_maximum_fusion.1), channel_id=1, source_target_pairs={{0,4},{4,8},{8,12},{1,5},{5,9},{9,13},{2,6},{6,10},{10,14},{3,7},{... | collective-permute-start | bytes 3145736 | tf_op jit(solution)/shard_map/ppermute | solution.py:35
  254.6 177.0 %collective-permute-start.5 = (bf16[512,1024]{0,1:T(8,128)(2,1)S(1)}, bf16[512,1024]{0,1:T(8,128)(2,1)S(1)}, u32[]{:S(2)}, u32[]{:S(2)}) collective-permute-start(bf16[512,1024]{0,1:T(8,128)(2,1)S(1)} %pad_maximum_fusion.1), channel_id=1, source_target_pairs={{0,8},{4,12},{1,9},{5,13},{2,10},{6,14},{3,11},{7,15},{16,24},{20,... | collective-permute-start | bytes 3145736 | tf_op jit(solution)/shard_map/ppermute | solution.py:35
  513.0 1.4 copy-start.8
  516.4 1.4 copy-start.3
  516.4 1.6 copy-start.5
  518.0 11.4 %copy-start.2 = (bf16[1536,512]{0,1:T(8,128)(2,1)S(1)}, bf16[1536,512]{0,1:T(8,128)(2,1)}, u32[]{:S(2)}) copy-start(bf16[1536,512]{0,1:T(8,128)(2,1)} %get-tuple-element.40) | copy-start | bytes 4718596
Sparse Core Ops, SparseCore 0:
  64.5 18.4 all-gather.3
  84.6 161.2 all-gather.5
  247.4 255.1 all-gather.7
